TPU v7x, 256 devices: a whole 4x4x8 slice. The times are simulated.
256 devices in a mesh: seg: 2 (over core), row: 128 (over z, y, x).
Axes of the slice: x: 4, y: 4, z: 8, core: 2. Of those that a mesh axis runs over, the one named last changes fastest.
Arguments:
- site_tensors: bfloat16 [4, 128, 4, 384, 384], P('seg', 'row'), may hold values from -1.5 to 1.5, as said below
- block_counts: int32 [4, 128], replicated, may hold values from 1 to 3, 256 in all within a row
- gate_even: float32 [16, 16], replicated, may hold values from -0.4 to 1.4, as said below
- gate_odd: float32 [16, 16], replicated, may hold values from -0.4 to 1.4, as said below
Outputs:
- evolved: bfloat16 [4, 128, 4, 384, 384], P('seg', 'row')
Inputs may be any that keep to these rules, and one draw needn't show every extreme that they name: block_counts[i, c] counts the live blocks of 128 rows of sector c on the bond left of site i; each row of block_counts sums to 256. `site_tensors`: entries in padded rows and columns are ignored. `gate_even`: only entries that conserve the charge are used. `gate_odd`: only entries that conserve the charge are used.
All inputs are finite; a program needn't handle non-finite values. Where the computation divides by a largest or mean magnitude, that divisor is 1e-20 or more.
Results may differ from a plain program's by a relative error of at most 0.008.
Values may be sent and summed in bfloat16 or wider, within the bound.
A program may use at most 128 MiB of HBM per device.

v0:
```python
import jax
import jax.numpy as jnp
import numpy as np
from jax import lax
from jax.sharding import PartitionSpec as P

BLOCK = 128
SWEEPS = 6


CHARGE_SHIFT = (-1, 0, 0, 1)
HIGHEST = lax.Precision.HIGHEST


def with_halo(block, sides, width):
    for axis, dim in sides:
        count = lax.axis_size(axis)
        forward = [(i, i + 1) for i in range(count - 1)]
        backward = [(target, source) for source, target in forward]
        low = lax.ppermute(
            lax.slice_in_dim(block, block.shape[dim] - width, None, axis=dim), axis, forward
        )
        high = lax.ppermute(lax.slice_in_dim(block, 0, width, axis=dim), axis, backward)
        block = jnp.concatenate([low, block, high], axis=dim)
    return block


def passed_along(value, axis, steps):
    count = lax.axis_size(axis)
    leading, last = (max(0, -steps), min(count, count - steps))
    return lax.ppermute(value, axis, [(source, source + steps) for source in range(leading, last)])


def conserving():
    charge = np.array(CHARGE_SHIFT)
    summed = (charge[:, None] + charge[None, :]).reshape(-1)
    return jnp.asarray((summed[:, None] == summed[None, :]).astype(np.float32))


def inverse_root(gram_matrix):
    row_count = gram_matrix.shape[-1]
    identity = jnp.eye(row_count, dtype=gram_matrix.dtype)
    widest = jnp.max(jnp.sum(jnp.abs(gram_matrix), axis=-1), axis=-1)
    current = gram_matrix / widest[..., None, None]
    factor = identity
    for sweep in range(SWEEPS):
        step_matrix = 0.5 * (3.0 * identity - jnp.matmul(factor, current, precision=HIGHEST))
        current = jnp.matmul(current, step_matrix, precision=HIGHEST)
        factor = jnp.matmul(step_matrix, factor, precision=HIGHEST)
    return factor / jnp.sqrt(widest)[..., None, None]


def count_row(block_counts, site_index):
    return lax.dynamic_index_in_dim(block_counts, site_index, 0, keepdims=False)


def pick_entry(count_list, wanted):
    return jnp.sum(
        jnp.where(jnp.arange(count_list.shape[0], dtype=jnp.int32) == wanted, count_list, 0)
    )


def local_mask(tensor, block_counts, site_index, sector):
    site_count = block_counts.shape[0]
    row_count = tensor.shape[-1]
    slot_index = jnp.arange(row_count, dtype=jnp.int32) // BLOCK
    left_row = count_row(block_counts, site_index)
    right_row = count_row(block_counts, (site_index + 1) % site_count)
    row_live = slot_index < pick_entry(left_row, sector)
    targets = sector + jnp.array(CHARGE_SHIFT, jnp.int32)
    onehot = jnp.arange(right_row.shape[0], dtype=jnp.int32)[None, :] == targets[:, None]
    col_count = jnp.sum(jnp.where(onehot, right_row[None, :], 0), axis=1)
    col_live = slot_index[None, :] < col_count[:, None]
    keep = row_live[None, :, None] & col_live[:, None, :]
    return jnp.where(keep, tensor, jnp.zeros_like(tensor))


def bond_update(left_tensor, right_tensor, layer_gate, mid_count):
    row_count = left_tensor.shape[-1]
    beside = with_halo(right_tensor[None], (("row", 0),), 1)
    partner = jnp.stack([beside[1 + CHARGE_SHIFT[s]] for s in range(4)])
    theta = jnp.einsum("sab,stbd->stad", left_tensor, partner, preferred_element_type=jnp.float32)
    gate_used = layer_gate * conserving()
    mixed_flat = jnp.einsum(
        "kj,jad->kad", gate_used, theta.reshape(16, row_count, row_count), precision=HIGHEST
    )
    mixed_blocks = mixed_flat.astype(jnp.bfloat16).reshape(4, 4, row_count, row_count)
    projected = jnp.einsum(
        "tuab,tuxb->tax", mixed_blocks, partner, preferred_element_type=jnp.float32
    )
    partial_grams = jnp.einsum("tam,tan->tmn", projected, projected, precision=HIGHEST)
    edge_grams = with_halo(
        jnp.stack([partial_grams[0], partial_grams[3]]).astype(jnp.bfloat16), (("row", 0),), 1
    ).astype(jnp.float32)
    slot_index = jnp.arange(row_count, dtype=jnp.int32) // BLOCK
    padding = (slot_index >= mid_count).astype(jnp.float32)
    identity = jnp.eye(row_count, dtype=jnp.float32)
    gram_matrix = (
        partial_grams[1]
        + partial_grams[2]
        + edge_grams[0]
        + edge_grams[3]
        + padding[:, None] * identity
    )
    inverse = inverse_root(gram_matrix)
    factor_beside = with_halo(inverse[None], (("row", 0),), 1)
    factor_stack = jnp.stack([factor_beside[1 + CHARGE_SHIFT[t]] for t in range(4)])
    new_left = jnp.einsum("tab,tbd->tad", projected, factor_stack, precision=HIGHEST).astype(
        jnp.bfloat16
    )
    right_terms = jnp.einsum(
        "tam,tuab->tumb", new_left, mixed_blocks, preferred_element_type=jnp.float32
    )
    right_terms = lax.optimization_barrier(right_terms.astype(jnp.bfloat16))
    arrived = with_halo(jnp.stack([right_terms[0], right_terms[3]]), (("row", 0),), 1)
    summed = right_terms[1].astype(jnp.float32) + right_terms[2].astype(jnp.float32)
    summed = summed + arrived[0].astype(jnp.float32) + arrived[3].astype(jnp.float32)
    return (new_left, summed.astype(jnp.bfloat16))


def body(site_tensors, block_counts, gate_even, gate_odd):
    local_count = site_tensors.shape[0]
    seg_index = lax.axis_index("seg")
    sector = lax.axis_index("row")
    seg_count = lax.axis_size("seg")
    site_count = block_counts.shape[0]
    first_site = seg_index * local_count
    current = [
        local_mask(site_tensors[j, 0], block_counts, first_site + j, sector)
        for j in range(local_count)
    ]
    for parity, layer_gate in ((0, gate_even), (1, gate_odd)):
        for left_slot in range(parity, local_count - 1, 2):
            mid_count = pick_entry(count_row(block_counts, first_site + left_slot + 1), sector)
            new_first, new_second = bond_update(
                current[left_slot], current[left_slot + 1], layer_gate, mid_count
            )
            current[left_slot] = new_first
            current[left_slot + 1] = new_second
    last_slot = local_count - 1
    is_left = seg_index + 1 < seg_count
    is_right = seg_index >= 1
    from_right = passed_along(current[0], "seg", -1)
    bond_site = (first_site + local_count) % site_count
    mid_count = pick_entry(count_row(block_counts, bond_site), sector)
    new_first, new_second = bond_update(current[last_slot], from_right, gate_odd, mid_count)
    returned = passed_along(new_second, "seg", 1)
    current[last_slot] = jnp.where(is_left, new_first, current[last_slot])
    current[0] = jnp.where(is_right, returned, current[0])
    return jnp.stack(current)[:, None]


def solution(mesh):
    in_specs = (P("seg", "row", None, None, None), P(), P(), P())
    out_specs = P("seg", "row", None, None, None)
    return jax.shard_map(body, mesh=mesh, in_specs=in_specs, out_specs=out_specs, check_vma=False)
```

profile of v0, /device:TPU:127, one launch (start us, length us, event | category | flops | bytes accessed | tf_op | source)
XLA Modules:
  0.0 405.5 jit_solution(3522867493047503054)
XLA Ops:
  7.6 4.3 %collective-permute-start = (bf16[1,4,384,384]{2,3,1,0:T(8,128)(2,1)S(1)}, bf16[1,4,384,384]{2,3,1,0:T(8,128)(2,1)S(1)}, u32[]{:S(2)}, u32[]{:S(2)}) collective-permute-start(bf16[1,4,384,384]{2,3,1,0:T(8,128)(2,1)S(1)} %and_select_fusion.1), channel_id=1, source_target_pairs={{0,1},{1,2},{2,3},{3,4},{4,5},{5,6},{6,7},{7,8},{8,9},{9,10},{10,1... | collective-permute-start | bytes 3538952 | tf_op jit(solution)/shard_map/ppermute | solution.py:20
  14.6 22.0 %collective-permute-done = bf16[1,4,384,384]{2,3,1,0:T(8,128)(2,1)S(1)} collective-permute-done((bf16[1,4,384,384]{2,3,1,0:T(8,128)(2,1)S(1)}, bf16[1,4,384,384]{2,3,1,0:T(8,128)(2,1)S(1)}, u32[]{:S(2)}, u32[]{:S(2)}) %collective-permute-start) | collective-permute-done | bytes 1179680 | tf_op jit(solution)/shard_map/ppermute | solution.py:20
  36.5 9.2 %collective-permute-done.1 = bf16[1,4,384,384]{2,3,1,0:T(8,128)(2,1)S(1)} collective-permute-done((bf16[1,4,384,384]{2,3,1,0:T(8,128)(2,1)S(1)}, bf16[1,4,384,384]{2,3,1,0:T(8,128)(2,1)S(1)}, u32[]{:S(2)}, u32[]{:S(2)}) %collective-permute-start.1) | collective-permute-done | bytes 1179680 | tf_op jit(solution)/shard_map/ppermute | solution.py:23
  45.8 7.2 %fusion.35 = f32[4,4,384,384]{3,2,1,0:T(8,128)} fusion(bf16[1,4,384,384]{2,3,1,0:T(8,128)(2,1)S(1)} %collective-permute-done.1, bf16[1,4,384,384]{2,3,1,0:T(8,128)(2,1)S(1)} %and_select_fusion.1, bf16[1,4,384,384]{2,3,1,0:T(8,128)(2,1)S(1)} %collective-permute-done, bf16[2,1,4,384,384]{4,3,2,1,0:T(8,128)(2,1)S(1)} %copy-done, ...), kind=kOutput, calls=%fused_computation.50 | convolution fusion | flops 1820196864 | bytes 14157824 | tf_op jit(solution)/shard_map/sab,stbd->stad/dot_general | solution.py:82
  53.0 9.8 %copy.34 = f32[16,384,384]{2,0,1:T(8,128)} copy(f32[16,384,384]{1,2,0:T(8,128)} %bitcast.185) | data formatting | bytes 18874368 | tf_op jit(solution)/shard_map/reshape | solution.py:85
  62.9 12.3 %convolution_convert_fusion.1 = bf16[16,384,384]{2,0,1:T(8,128)(2,1)} fusion(f32[16,384,384]{2,0,1:T(8,128)} %copy.34, f32[16,16]{1,0:T(8,128)S(1)} %copy-done.7, f32[16,16]{1,0:T(8,128)S(1)} %copy-done.6), kind=kOutput, calls=%fused_computation.5 | convolution fusion | flops 455344384 | bytes 14157824 | tf_op jit(solution)/shard_map/kj,jad->kad/dot_general | solution.py:84
  75.2 7.3 %copy.80 = bf16[16,384,384]{1,2,0:T(8,128)(2,1)} copy(bf16[16,384,384]{2,0,1:T(8,128)(2,1)} %convolution_convert_fusion.1) | data formatting | bytes 9437184 | tf_op jit(solution)/shard_map/reshape | solution.py:87
  82.5 5.3 %fusion.34 = f32[4,384,384,1]{2,1,3,0:T(8,128)S(1)} fusion(bf16[4,4,384,384]{2,3,1,0:T(8,128)(2,1)} %bitcast.177, bf16[1,4,384,384]{2,3,1,0:T(8,128)(2,1)} %copy-done.13, bf16[1,4,384,384]{2,3,1,0:T(8,128)(2,1)S(1)} %and_select_fusion.1, bf16[1,4,384,384]{2,3,1,0:T(8,128)(2,1)S(1)} %copy-done.12), kind=kOutput, calls=%fused_computation.49 | convolution fusion | flops 1819017216 | bytes 10616832 | tf_op jit(solution)/shard_map/tuab,tuxb->tax/dot_general | solution.py:88
  87.9 4.9 %fusion.101 = (bf16[4,384,384]{1,2,0:T(8,128)(2,1)S(1)}, f32[4,384,384]{1,2,0:T(8,128)S(1)}) fusion(f32[4,384,384,1]{2,1,3,0:T(8,128)S(1)} %fusion.34), kind=kOutput, calls=%fused_computation.151 | convolution fusion | flops 2718498816 | bytes 5898240 | tf_op jit(solution)/shard_map/tam,tan->tmn/dot_general | solution.py:91
  94.7 3.8 collective-permute-start.3
  101.3 7.4 %collective-permute-done.3 = bf16[1,384,384]{1,2,0:T(8,128)(2,1)S(1)} collective-permute-done((bf16[1,384,384]{1,2,0:T(8,128)(2,1)S(1)}, bf16[1,384,384]{1,2,0:T(8,128)(2,1)S(1)}, u32[]{:S(2)}, u32[]{:S(2)}) %collective-permute-start.3) | collective-permute-done | bytes 294944 | tf_op jit(solution)/shard_map/ppermute | solution.py:23
  140.1 8.4 %collective-permute-done.4 = f32[1,384,384]{2,1,0:T(8,128)S(1)} collective-permute-done((f32[1,384,384]{2,1,0:T(8,128)S(1)}, f32[1,384,384]{2,1,0:T(8,128)S(1)}, u32[]{:S(2)}, u32[]{:S(2)}) %collective-permute-start.4) | collective-permute-done | bytes 589856 | tf_op jit(solution)/shard_map/ppermute | solution.py:20
  148.5 7.4 %collective-permute-done.5 = f32[1,384,384]{2,1,0:T(8,128)S(1)} collective-permute-done((f32[1,384,384]{2,1,0:T(8,128)S(1)}, f32[1,384,384]{2,1,0:T(8,128)S(1)}, u32[]{:S(2)}, u32[]{:S(2)}) %collective-permute-start.5) | collective-permute-done | bytes 589856 | tf_op jit(solution)/shard_map/ppermute | solution.py:23
  155.8 4.6 %fusion.27 = bf16[4,384,384]{2,1,0:T(8,128)(2,1)S(1)} fusion(f32[1,384,384]{2,1,0:T(8,128)S(1)} %collective-permute-done.5, f32[1,384,384]{2,1,0:T(8,128)S(1)} %fusion.36, f32[1,384,384]{2,1,0:T(8,128)S(1)} %collective-permute-done.4, f32[4,384,384,1]{2,1,3,0:T(8,128)S(1)} %copy-done.5), kind=kOutput, calls=%fused_computation.46 | convolution fusion | flops 2720268288 | bytes 5308416 | tf_op jit(solution)/shard_map/tab,tbd->tad/dot_general | solution.py:108
  160.5 5.7 %collective-permute-start.6 = (bf16[4,384,384]{2,1,0:T(8,128)(2,1)S(1)}, bf16[4,384,384]{2,1,0:T(8,128)(2,1)S(1)}, u32[]{:S(2)}, u32[]{:S(2)}) collective-permute-start(bf16[4,384,384]{2,1,0:T(8,128)(2,1)S(1)} %fusion.27), channel_id=1, source_target_pairs={{128,0},{129,1},{130,2},{131,3},{132,4},{133,5},{134,6},{135,7},{1... | collective-permute-start | bytes 3538952 | tf_op jit(solution)/shard_map/ppermute | solution.py:31
  171.3 8.8 %collective-permute-start.9 = (bf16[1,4,384,384]{3,2,1,0:T(8,128)(2,1)S(1)}, bf16[1,4,384,384]{3,2,1,0:T(8,128)(2,1)S(1)}, u32[]{:S(2)}, u32[]{:S(2)}) collective-permute-start(bf16[1,4,384,384]{3,2,1,0:T(8,128)(2,1)S(1)} %get-tuple-element.17), channel_id=1, source_target_pairs={{0,1},{1,2},{2,3},{3,4},{4,5},{5,6},{6,7},{7,8},{8,9},{9,10},{10,1... | collective-permute-start | bytes 3538952 | tf_op jit(solution)/shard_map/ppermute | solution.py:20
  185.7 19.0 %collective-permute-done.10 = bf16[1,4,384,384]{3,2,1,0:T(8,128)(2,1)S(1)} collective-permute-done((bf16[1,4,384,384]{3,2,1,0:T(8,128)(2,1)S(1)}, bf16[1,4,384,384]{3,2,1,0:T(8,128)(2,1)S(1)}, u32[]{:S(2)}, u32[]{:S(2)}) %collective-permute-start.10) | collective-permute-done | bytes 1179680 | tf_op jit(solution)/shard_map/ppermute | solution.py:23
  206.4 24.6 %collective-permute-done.7 = bf16[1,4,384,384]{3,2,1,0:T(8,128)(2,1)S(1)} collective-permute-done((bf16[1,4,384,384]{3,2,1,0:T(8,128)(2,1)S(1)}, bf16[1,4,384,384]{3,2,1,0:T(8,128)(2,1)S(1)}, u32[]{:S(2)}, u32[]{:S(2)}) %collective-permute-start.7) | collective-permute-done | bytes 1179680 | tf_op jit(solution)/shard_map/ppermute | solution.py:20
  231.1 6.0 %fusion.33 = f32[4,4,384,384]{3,2,1,0:T(8,128)} fusion(bf16[1,4,384,384]{3,2,1,0:T(8,128)(2,1)S(1)} %collective-permute-done.8, bf16[1,4,384,384]{3,2,1,0:T(8,128)(2,1)S(1)} %bitcast.189, bf16[1,4,384,384]{3,2,1,0:T(8,128)(2,1)S(1)} %collective-permute-done.7, bf16[1,4,384,384]{3,2,1,0:T(8,128)(2,1)S(1)} %add_convert_fusion.1), kind=kOutput, calls=%fused_computation.48 | convolution fusion | flops 1819017216 | bytes 14155776 | tf_op jit(solution)/shard_map/sab,stbd->stad/dot_general | solution.py:82
  237.1 9.8 %copy.46 = f32[16,384,384]{2,0,1:T(8,128)} copy(f32[16,384,384]{1,2,0:T(8,128)} %bitcast.186) | data formatting | bytes 18874368 | tf_op jit(solution)/shard_map/reshape | solution.py:85
  247.0 12.3 %convolution_convert_fusion = bf16[16,384,384]{2,0,1:T(8,128)(2,1)} fusion(f32[16,384,384]{2,0,1:T(8,128)} %copy.46, f32[16,16]{1,0:T(8,128)S(1)} %copy-done.8, f32[16,16]{1,0:T(8,128)S(1)} %copy-done.6), kind=kOutput, calls=%fused_computation.4 | convolution fusion | flops 455344384 | bytes 14157824 | tf_op jit(solution)/shard_map/kj,jad->kad/dot_general | solution.py:84
  259.3 7.5 %copy.81 = bf16[16,384,384]{1,2,0:T(8,128)(2,1)} copy(bf16[16,384,384]{2,0,1:T(8,128)(2,1)} %convolution_convert_fusion) | data formatting | bytes 9437184 | tf_op jit(solution)/shard_map/reshape | solution.py:87
  266.8 6.1 %fusion.32 = f32[4,384,384,1]{2,1,3,0:T(8,128)S(1)} fusion(bf16[4,4,384,384]{2,3,1,0:T(8,128)(2,1)} %bitcast.181, bf16[1,4,384,384]{3,2,1,0:T(8,128)(2,1)} %copy-done.10, bf16[1,4,384,384]{3,2,1,0:T(8,128)(2,1)S(1)} %bitcast.190, bf16[1,4,384,384]{3,2,1,0:T(8,128)(2,1)} %copy-done.9), kind=kOutput, calls=%fused_computation.47 | convolution fusion | flops 1819017216 | bytes 10616832 | tf_op jit(solution)/shard_map/tuab,tuxb->tax/dot_general | solution.py:88
  272.9 5.0 %fusion.102 = (bf16[4,384,384]{1,2,0:T(8,128)(2,1)S(1)}, f32[4,384,384]{1,2,0:T(8,128)S(1)}) fusion(f32[4,384,384,1]{2,1,3,0:T(8,128)S(1)} %fusion.32), kind=kOutput, calls=%fused_computation.152 | convolution fusion | flops 2718498816 | bytes 5898240 | tf_op jit(solution)/shard_map/tam,tan->tmn/dot_general | solution.py:91
  278.0 9.5 %collective-permute-start.11 = (bf16[1,384,384]{1,2,0:T(8,128)(2,1)S(1)}, bf16[1,384,384]{1,2,0:T(8,128)(2,1)S(1)}, u32[]{:S(2)}, u32[]{:S(2)}) collective-permute-start(bf16[1,384,384]{1,2,0:T(8,128)(2,1)S(1)} %get-tuple-element.19), channel_id=1, source_target_pairs={{0,1},{1,2},{2,3},{3,4},{4,5},{5,6},{6,7},{7,8},{8,9},{9,10},{10,1... | collective-permute-start | bytes 884744 | tf_op jit(solution)/shard_map/ppermute | solution.py:20
  293.4 9.2 %collective-permute-done.12 = bf16[1,384,384]{1,2,0:T(8,128)(2,1)S(1)} collective-permute-done((bf16[1,384,384]{1,2,0:T(8,128)(2,1)S(1)}, bf16[1,384,384]{1,2,0:T(8,128)(2,1)S(1)}, u32[]{:S(2)}, u32[]{:S(2)}) %collective-permute-start.12) | collective-permute-done | bytes 294944 | tf_op jit(solution)/shard_map/ppermute | solution.py:23
  334.1 9.5 %collective-permute-done.13 = f32[1,384,384]{2,1,0:T(8,128)S(1)} collective-permute-done((f32[1,384,384]{2,1,0:T(8,128)S(1)}, f32[1,384,384]{2,1,0:T(8,128)S(1)}, u32[]{:S(2)}, u32[]{:S(2)}) %collective-permute-start.13) | collective-permute-done | bytes 589856 | tf_op jit(solution)/shard_map/ppermute | solution.py:20
  343.6 7.4 %collective-permute-done.14 = f32[1,384,384]{2,1,0:T(8,128)S(1)} collective-permute-done((f32[1,384,384]{2,1,0:T(8,128)S(1)}, f32[1,384,384]{2,1,0:T(8,128)S(1)}, u32[]{:S(2)}, u32[]{:S(2)}) %collective-permute-start.14) | collective-permute-done | bytes 589856 | tf_op jit(solution)/shard_map/ppermute | solution.py:23
  351.0 4.6 %fusion.22 = bf16[4,384,384]{2,1,0:T(8,128)(2,1)S(1)} fusion(f32[1,384,384]{2,1,0:T(8,128)S(1)} %collective-permute-done.14, f32[1,384,384]{2,1,0:T(8,128)S(1)} %fusion.37, f32[1,384,384]{2,1,0:T(8,128)S(1)} %collective-permute-done.13, f32[4,384,384,1]{2,1,3,0:T(8,128)S(1)} %copy-done.3), kind=kOutput, calls=%fused_computation.45 | convolution fusion | flops 2720268288 | bytes 5308416 | tf_op jit(solution)/shard_map/tab,tbd->tad/dot_general | solution.py:108
  364.1 21.5 %collective-permute-done.15 = bf16[1,4,384,384]{3,2,1,0:T(8,128)(2,1)S(1)} collective-permute-done((bf16[1,4,384,384]{3,2,1,0:T(8,128)(2,1)S(1)}, bf16[1,4,384,384]{3,2,1,0:T(8,128)(2,1)S(1)}, u32[]{:S(2)}, u32[]{:S(2)}) %collective-permute-start.15) | collective-permute-done | bytes 1179680 | tf_op jit(solution)/shard_map/ppermute | solution.py:20
  385.6 7.4 %collective-permute-done.16 = bf16[1,4,384,384]{3,2,1,0:T(8,128)(2,1)S(1)} collective-permute-done((bf16[1,4,384,384]{3,2,1,0:T(8,128)(2,1)S(1)}, bf16[1,4,384,384]{3,2,1,0:T(8,128)(2,1)S(1)}, u32[]{:S(2)}, u32[]{:S(2)}) %collective-permute-start.16) | collective-permute-done | bytes 1179680 | tf_op jit(solution)/shard_map/ppermute | solution.py:23
  397.3 4.7 %collective-permute-done.17 = bf16[4,384,384]{2,1,0:T(8,128)(2,1)} collective-permute-done((bf16[4,384,384]{2,1,0:T(8,128)(2,1)}, bf16[4,384,384]{2,1,0:T(8,128)(2,1)}, u32[]{:S(2)}, u32[]{:S(2)}) %collective-permute-start.17) | collective-permute-done | bytes 1179680 | tf_op jit(solution)/shard_map/ppermute | solution.py:31
  (119 shorter events, 110.3 us)
Async XLA Ops:
  4.2 41.6 %copy-start = (bf16[2,1,4,384,384]{4,3,2,1,0:T(8,128)(2,1)S(1)}, bf16[2,1,4,384,384]{4,3,2,1,0:T(8,128)(2,1)}, u32[]{:S(2)}) copy-start(bf16[2,1,4,384,384]{4,3,2,1,0:T(8,128)(2,1)} %param.8) | copy-start | bytes 7077892
  7.6 29.0 %collective-permute-start = (bf16[1,4,384,384]{2,3,1,0:T(8,128)(2,1)S(1)}, bf16[1,4,384,384]{2,3,1,0:T(8,128)(2,1)S(1)}, u32[]{:S(2)}, u32[]{:S(2)}) collective-permute-start(bf16[1,4,384,384]{2,3,1,0:T(8,128)(2,1)S(1)} %and_select_fusion.1), channel_id=1, source_target_pairs={{0,1},{1,2},{2,3},{3,4},{4,5},{5,6},{6,7},{7,8},{8,9},{9,10},{10,1... | collective-permute-start | bytes 3538952 | tf_op jit(solution)/shard_map/ppermute | solution.py:20
  11.9 33.8 %collective-permute-start.1 = (bf16[1,4,384,384]{2,3,1,0:T(8,128)(2,1)S(1)}, bf16[1,4,384,384]{2,3,1,0:T(8,128)(2,1)S(1)}, u32[]{:S(2)}, u32[]{:S(2)}) collective-permute-start(bf16[1,4,384,384]{2,3,1,0:T(8,128)(2,1)S(1)} %and_select_fusion.1), channel_id=1, source_target_pairs={{1,0},{2,1},{3,2},{4,3},{5,4},{6,5},{7,6},{8,7},{9,8},{10,9},{11,1... | collective-permute-start | bytes 3538952 | tf_op jit(solution)/shard_map/ppermute | solution.py:23
  36.5 16.5 %copy-start.11 = (bf16[1,4,384,384]{2,3,1,0:T(8,128)(2,1)}, bf16[1,4,384,384]{2,3,1,0:T(8,128)(2,1)S(1)}, u32[]{:S(2)}) copy-start(bf16[1,4,384,384]{2,3,1,0:T(8,128)(2,1)S(1)} %collective-permute-done) | copy-start | bytes 3538948
  45.8 7.2 %copy-start.13 = (bf16[1,4,384,384]{2,3,1,0:T(8,128)(2,1)}, bf16[1,4,384,384]{2,3,1,0:T(8,128)(2,1)S(1)}, u32[]{:S(2)}) copy-start(bf16[1,4,384,384]{2,3,1,0:T(8,128)(2,1)S(1)} %collective-permute-done.1) | copy-start | bytes 3538948
  53.0 9.9 %copy-start.6 = (f32[16,16]{1,0:T(8,128)S(1)}, f32[16,16]{1,0:T(8,128)}, u32[]{:S(2)}) copy-start(f32[16,16]{1,0:T(8,128)} %constant.98.clone) | copy-start | bytes 3076
  53.0 9.9 %copy-start.7 = (f32[16,16]{1,0:T(8,128)S(1)}, f32[16,16]{1,0:T(8,128)}, u32[]{:S(2)}) copy-start(f32[16,16]{1,0:T(8,128)} %param.10) | copy-start | bytes 3076
  75.2 7.3 %copy-start.12 = (bf16[1,4,384,384]{2,3,1,0:T(8,128)(2,1)S(1)}, bf16[1,4,384,384]{2,3,1,0:T(8,128)(2,1)}, u32[]{:S(2)}) copy-start(bf16[1,4,384,384]{2,3,1,0:T(8,128)(2,1)} %copy-done.11) | copy-start | bytes 3538948
  92.8 8.5 %collective-permute-start.2 = (bf16[1,384,384]{1,2,0:T(8,128)(2,1)S(1)}, bf16[1,384,384]{1,2,0:T(8,128)(2,1)S(1)}, u32[]{:S(2)}, u32[]{:S(2)}) collective-permute-start(bf16[1,384,384]{1,2,0:T(8,128)(2,1)S(1)} %get-tuple-element.21), channel_id=1, source_target_pairs={{0,1},{1,2},{2,3},{3,4},{4,5},{5,6},{6,7},{7,8},{8,9},{9,10},{10,1... | collective-permute-start | bytes 884744 | tf_op jit(solution)/shard_map/ppermute | solution.py:20
  94.7 14.0 %collective-permute-start.3 = (bf16[1,384,384]{1,2,0:T(8,128)(2,1)S(1)}, bf16[1,384,384]{1,2,0:T(8,128)(2,1)S(1)}, u32[]{:S(2)}, u32[]{:S(2)}) collective-permute-start(bf16[1,384,384]{1,2,0:T(8,128)(2,1)S(1)} %get-tuple-element.22), channel_id=1, source_target_pairs={{1,0},{2,1},{3,2},{4,3},{5,4},{6,5},{7,6},{8,7},{9,8},{10,9},{11,1... | collective-permute-start | bytes 884744 | tf_op jit(solution)/shard_map/ppermute | solution.py:23
  129.7 36.5 %slice-start = ((s8[4718592]{0:T(1024)(128)(4,1)}), s8[524288]{0:T(1024)(128)(4,1)S(1)}, s32[]{:S(2)}) async-start(s8[4718592]{0:T(1024)(128)(4,1)} %bitcast.178), calls=%async_computation | async-start | bytes 1048576
  131.7 24.1 %copy-start.5 = (f32[4,384,384,1]{2,1,3,0:T(8,128)S(1)}, f32[4,384,384,1]{2,1,3,0:T(8,128)}, u32[]{:S(2)}) copy-start(f32[4,384,384,1]{2,1,3,0:T(8,128)} %copy-done.4) | copy-start | bytes 7077892
  133.1 33.1 %slice-start.1 = ((s8[4718592]{0:T(1024)(128)(4,1)}), s8[4194304]{0:T(1024)(128)(4,1)S(1)}, s32[]{:S(2)}) async-start(s8[4718592]{0:T(1024)(128)(4,1)} %bitcast.178), calls=%async_computation.1 | async-start | bytes 8388608
  134.6 13.9 %collective-permute-start.4 = (f32[1,384,384]{2,1,0:T(8,128)S(1)}, f32[1,384,384]{2,1,0:T(8,128)S(1)}, u32[]{:S(2)}, u32[]{:S(2)}) collective-permute-start(f32[1,384,384]{2,1,0:T(8,128)S(1)} %fusion.36), channel_id=1, source_target_pairs={{0,1},{1,2},{2,3},{3,4},{4,5},{5,6},{6,7},{7,8},{8,9},{9,10},{10,1... | collective-permute-start | bytes 1769480 | tf_op jit(solution)/shard_map/ppermute | solution.py:20
  136.5 19.3 %collective-permute-start.5 = (f32[1,384,384]{2,1,0:T(8,128)S(1)}, f32[1,384,384]{2,1,0:T(8,128)S(1)}, u32[]{:S(2)}, u32[]{:S(2)}) collective-permute-start(f32[1,384,384]{2,1,0:T(8,128)S(1)} %fusion.36), channel_id=1, source_target_pairs={{1,0},{2,1},{3,2},{4,3},{5,4},{6,5},{7,6},{8,7},{9,8},{10,9},{11,1... | collective-permute-start | bytes 1769480 | tf_op jit(solution)/shard_map/ppermute | solution.py:23
  160.5 19.6 %collective-permute-start.6 = (bf16[4,384,384]{2,1,0:T(8,128)(2,1)S(1)}, bf16[4,384,384]{2,1,0:T(8,128)(2,1)S(1)}, u32[]{:S(2)}, u32[]{:S(2)}) collective-permute-start(bf16[4,384,384]{2,1,0:T(8,128)(2,1)S(1)} %fusion.27), channel_id=1, source_target_pairs={{128,0},{129,1},{130,2},{131,3},{132,4},{133,5},{134,6},{135,7},{1... | collective-permute-start | bytes 3538952 | tf_op jit(solution)/shard_map/ppermute | solution.py:31
  169.4 35.3 %collective-permute-start.10 = (bf16[1,4,384,384]{3,2,1,0:T(8,128)(2,1)S(1)}, bf16[1,4,384,384]{3,2,1,0:T(8,128)(2,1)S(1)}, u32[]{:S(2)}, u32[]{:S(2)}) collective-permute-start(bf16[1,4,384,384]{3,2,1,0:T(8,128)(2,1)S(1)} %get-tuple-element.18), channel_id=1, source_target_pairs={{1,0},{2,1},{3,2},{4,3},{5,4},{6,5},{7,6},{8,7},{9,8},{10,9},{11,1... | collective-permute-start | bytes 3538952 | tf_op jit(solution)/shard_map/ppermute | solution.py:23
  171.3 34.5 %collective-permute-start.9 = (bf16[1,4,384,384]{3,2,1,0:T(8,128)(2,1)S(1)}, bf16[1,4,384,384]{3,2,1,0:T(8,128)(2,1)S(1)}, u32[]{:S(2)}, u32[]{:S(2)}) collective-permute-start(bf16[1,4,384,384]{3,2,1,0:T(8,128)(2,1)S(1)} %get-tuple-element.17), channel_id=1, source_target_pairs={{0,1},{1,2},{2,3},{3,4},{4,5},{5,6},{6,7},{7,8},{8,9},{9,10},{10,1... | collective-permute-start | bytes 3538952 | tf_op jit(solution)/shard_map/ppermute | solution.py:20
  180.1 51.0 %collective-permute-start.7 = (bf16[1,4,384,384]{3,2,1,0:T(8,128)(2,1)S(1)}, bf16[1,4,384,384]{3,2,1,0:T(8,128)(2,1)S(1)}, u32[]{:S(2)}, u32[]{:S(2)}) collective-permute-start(bf16[1,4,384,384]{3,2,1,0:T(8,128)(2,1)S(1)} %bitcast.187), channel_id=1, source_target_pairs={{0,1},{1,2},{2,3},{3,4},{4,5},{5,6},{6,7},{7,8},{8,9},{9,10},{10,1... | collective-permute-start | bytes 3538952 | tf_op jit(solution)/shard_map/ppermute | solution.py:20
  182.0 49.0 %collective-permute-start.8 = (bf16[1,4,384,384]{3,2,1,0:T(8,128)(2,1)S(1)}, bf16[1,4,384,384]{3,2,1,0:T(8,128)(2,1)S(1)}, u32[]{:S(2)}, u32[]{:S(2)}) collective-permute-start(bf16[1,4,384,384]{3,2,1,0:T(8,128)(2,1)S(1)} %bitcast.188), channel_id=1, source_target_pairs={{1,0},{2,1},{3,2},{4,3},{5,4},{6,5},{7,6},{8,7},{9,8},{10,9},{11,1... | collective-permute-start | bytes 3538952 | tf_op jit(solution)/shard_map/ppermute | solution.py:23
  206.4 30.7 %copy-start.1 = (bf16[1,4,384,384]{3,2,1,0:T(8,128)(2,1)}, bf16[1,4,384,384]{3,2,1,0:T(8,128)(2,1)S(1)}, u32[]{:S(2)}) copy-start(bf16[1,4,384,384]{3,2,1,0:T(8,128)(2,1)S(1)} %add_convert_fusion.1) | copy-start | bytes 3538948
  237.1 9.8 %copy-start.8 = (f32[16,16]{1,0:T(8,128)S(1)}, f32[16,16]{1,0:T(8,128)}, u32[]{:S(2)}) copy-start(f32[16,16]{1,0:T(8,128)} %param.11) | copy-start | bytes 3076
  278.0 15.4 %collective-permute-start.11 = (bf16[1,384,384]{1,2,0:T(8,128)(2,1)S(1)}, bf16[1,384,384]{1,2,0:T(8,128)(2,1)S(1)}, u32[]{:S(2)}, u32[]{:S(2)}) collective-permute-start(bf16[1,384,384]{1,2,0:T(8,128)(2,1)S(1)} %get-tuple-element.19), channel_id=1, source_target_pairs={{0,1},{1,2},{2,3},{3,4},{4,5},{5,6},{6,7},{7,8},{8,9},{9,10},{10,1... | collective-permute-start | bytes 884744 | tf_op jit(solution)/shard_map/ppermute | solution.py:20
  287.5 15.1 %collective-permute-start.12 = (bf16[1,384,384]{1,2,0:T(8,128)(2,1)S(1)}, bf16[1,384,384]{1,2,0:T(8,128)(2,1)S(1)}, u32[]{:S(2)}, u32[]{:S(2)}) collective-permute-start(bf16[1,384,384]{1,2,0:T(8,128)(2,1)S(1)} %get-tuple-element.20), channel_id=1, source_target_pairs={{1,0},{2,1},{3,2},{4,3},{5,4},{6,5},{7,6},{8,7},{9,8},{10,9},{11,1... | collective-permute-start | bytes 884744 | tf_op jit(solution)/shard_map/ppermute | solution.py:23
  323.7 32.0 %slice-start.2 = ((s8[4718592]{0:T(1024)(128)(4,1)}), s8[524288]{0:T(1024)(128)(4,1)S(1)}, s32[]{:S(2)}) async-start(s8[4718592]{0:T(1024)(128)(4,1)} %bitcast.182), calls=%async_computation.2 | async-start | bytes 1048576
  325.7 25.3 %copy-start.3 = (f32[4,384,384,1]{2,1,3,0:T(8,128)S(1)}, f32[4,384,384,1]{2,1,3,0:T(8,128)}, u32[]{:S(2)}) copy-start(f32[4,384,384,1]{2,1,3,0:T(8,128)} %copy-done.2) | copy-start | bytes 7077892
  327.1 28.5 %slice-start.3 = ((s8[4718592]{0:T(1024)(128)(4,1)}), s8[4194304]{0:T(1024)(128)(4,1)S(1)}, s32[]{:S(2)}) async-start(s8[4718592]{0:T(1024)(128)(4,1)} %bitcast.182), calls=%async_computation.3 | async-start | bytes 8388608
  328.5 15.1 %collective-permute-start.13 = (f32[1,384,384]{2,1,0:T(8,128)S(1)}, f32[1,384,384]{2,1,0:T(8,128)S(1)}, u32[]{:S(2)}, u32[]{:S(2)}) collective-permute-start(f32[1,384,384]{2,1,0:T(8,128)S(1)} %fusion.37), channel_id=1, source_target_pairs={{0,1},{1,2},{2,3},{3,4},{4,5},{5,6},{6,7},{7,8},{8,9},{9,10},{10,1... | collective-permute-start | bytes 1769480 | tf_op jit(solution)/shard_map/ppermute | solution.py:20
  330.5 20.5 %collective-permute-start.14 = (f32[1,384,384]{2,1,0:T(8,128)S(1)}, f32[1,384,384]{2,1,0:T(8,128)S(1)}, u32[]{:S(2)}, u32[]{:S(2)}) collective-permute-start(f32[1,384,384]{2,1,0:T(8,128)S(1)} %fusion.37), channel_id=1, source_target_pairs={{1,0},{2,1},{3,2},{4,3},{5,4},{6,5},{7,6},{8,7},{9,8},{10,9},{11,1... | collective-permute-start | bytes 1769480 | tf_op jit(solution)/shard_map/ppermute | solution.py:23
  358.8 26.8 %collective-permute-start.15 = (bf16[1,4,384,384]{3,2,1,0:T(8,128)(2,1)S(1)}, bf16[1,4,384,384]{3,2,1,0:T(8,128)(2,1)S(1)}, u32[]{:S(2)}, u32[]{:S(2)}) collective-permute-start(bf16[1,4,384,384]{3,2,1,0:T(8,128)(2,1)S(1)} %get-tuple-element.15), channel_id=1, source_target_pairs={{0,1},{1,2},{2,3},{3,4},{4,5},{5,6},{6,7},{7,8},{8,9},{9,10},{10,1... | collective-permute-start | bytes 3538952 | tf_op jit(solution)/shard_map/ppermute | solution.py:20
  360.7 32.2 %collective-permute-start.16 = (bf16[1,4,384,384]{3,2,1,0:T(8,128)(2,1)S(1)}, bf16[1,4,384,384]{3,2,1,0:T(8,128)(2,1)S(1)}, u32[]{:S(2)}, u32[]{:S(2)}) collective-permute-start(bf16[1,4,384,384]{3,2,1,0:T(8,128)(2,1)S(1)} %get-tuple-element.16), channel_id=1, source_target_pairs={{1,0},{2,1},{3,2},{4,3},{5,4},{6,5},{7,6},{8,7},{9,8},{10,9},{11,1... | collective-permute-start | bytes 3538952 | tf_op jit(solution)/shard_map/ppermute | solution.py:23
  394.6 7.4 %collective-permute-start.17 = (bf16[4,384,384]{2,1,0:T(8,128)(2,1)}, bf16[4,384,384]{2,1,0:T(8,128)(2,1)}, u32[]{:S(2)}, u32[]{:S(2)}) collective-permute-start(bf16[4,384,384]{2,1,0:T(8,128)(2,1)} %fusion.52), channel_id=1, source_target_pairs={{0,128},{1,129},{2,130},{3,131},{4,132},{5,133},{6,134},{7,135},{8... | collective-permute-start | bytes 3538952 | tf_op jit(solution)/shard_map/ppermute | solution.py:31
  (5 other events, 26.2 us)
where the time goes:
time: 414 us; the launch traced here: 406 us
  waiting for transfers between devices  164 us (40%)
  matrix products  123 us (30%)
  starting transfers between devices  63.1 us (15%)
  local copies, waits for them, and re-layouts  37.4 us (9%)
  other arithmetic  15.6 us (4%)
    ppermute x8, waiting for transfers between devices, with_halo(): lax.ppermute(lax.slice_in_dim(block, block.shape[dim] - width, None, axis...  92.6 us
    ppermute x8, waiting for transfers between devices, with_halo(): lax.ppermute(lax.slice_in_dim(block, 0, width, axis=dim), axis, backward)  66.9 us
    ppermute x8, starting transfers between devices, with_halo(): lax.ppermute(lax.slice_in_dim(block, block.shape[dim] - width, None, axis...  32.3 us
    dot_general x2, matrix products, bond_update(): jnp.einsum('kj,jad->kad', gate_used, theta.reshape(16, row_count, row_cou...  24.6 us
    ppermute x8, starting transfers between devices, with_halo(): lax.ppermute(lax.slice_in_dim(block, 0, width, axis=dim), axis, backward)  23.9 us
    reshape x2, local copies, waits for them, and re-layouts, bond_update(): theta.reshape(16, row_count, row_count)  19.7 us
    dot_general x12, matrix products, inverse_root(): jnp.matmul(factor, current, precision=HIGHEST)  16.5 us
    dot_general x12, matrix products, inverse_root(): factor = jnp.matmul(step_matrix, factor, precision=HIGHEST)  16.5 us
  transfers between devices with their start and end apart: 18, of which 16 were waited for; matrix products, arithmetic and copies ran while one was open for 2% of the time, Pallas kernels for 0%

commit v1 on v0

v1 whole, which is shorter than its diff:
```python
import functools

import jax
import jax.numpy as jnp
from jax import lax
from jax.experimental import pallas as pl
from jax.experimental.pallas import tpu as pltpu
from jax.sharding import PartitionSpec as P

MESH = pl.DeviceIdType.MESH
BF16, F32 = jnp.bfloat16, jnp.float32
BLOCK = 128
D = 384
SHIFT = (-1, 0, 0, 1)
ROWS = 16

MINUS = ((0, 1), (0, 2), (1, 0), (2, 0))
ZERO = ((0, 3), (1, 1), (1, 2), (2, 1), (2, 2), (3, 0))
PLUS = ((1, 3), (2, 3), (3, 1), (3, 2))


def dot(a, b):
    return jnp.dot(a, b, preferred_element_type=F32)


def dot_nt(a, b):
    return lax.dot_general(a, b, (((1,), (1,)), ((), ())), preferred_element_type=F32)


def split(x):
    high = x.astype(BF16)
    return high, (x - high.astype(F32)).astype(BF16)


def store_left(ref, x):
    high, low = split(x)
    ref[:, 0:D] = high
    ref[:, D : 2 * D] = low
    ref[:, 2 * D : 3 * D] = high


def store_right(ref, x, at):
    high, low = split(x)
    ref[0:D, at : at + D] = high
    ref[D : 2 * D, at : at + D] = high
    ref[2 * D : 3 * D, at : at + D] = low


def cols(s, count=1):
    return slice(s * D, (s + count) * D)


def kernel(x, counts, gate_even, gate_odd, out,
           left_m, right_m, halo_low, halo_high, edge_low, edge_high, send_0, send_3, mixed,
           returned, left_o, right_o, halo_low_o, halo_high_o, edge_low_o, edge_high_o,
           send_0o, send_3o, mixed_o, returned_o, right_new,
           theta_0, theta_12, theta_3, proj_r, new_t, new_l, new_lo, ns_s, ns_l, ns_g, ns_r, ns_q,
           send_sem, recv_sem):
    seg, row = lax.axis_index("seg"), lax.axis_index("row")
    rows = lax.axis_size("row")
    up, down = lax.rem(row + 1, rows), lax.rem(row + rows - 1, rows)
    first, last = row == 0, row == rows - 1

    barrier = pltpu.get_barrier_semaphore()
    for target in ((seg, up), (seg, down), (1 - seg, row), (1 - seg, up), (1 - seg, down)):
        pl.semaphore_signal(barrier, inc=1, device_id=target, device_id_type=MESH)

    def copy(k, src, dst, target):
        return pltpu.make_async_remote_copy(
            src_ref=src, dst_ref=dst, send_sem=send_sem.at[k], recv_sem=recv_sem.at[k],
            device_id=target, device_id_type=MESH,
        )

    def live(site, sector, block):
        inside = (sector >= 0) & (sector < rows)
        count = counts[site, jnp.clip(sector, 0, rows - 1)]
        return jnp.where(inside & (block < count), 1.0, 0.0).astype(F32)

    def mask(slot, store):
        site = 2 * seg + slot
        right_site = lax.rem(site + 1, 4)
        row_live = [live(site, row, i) for i in range(3)]
        for s in (1, 2, 0, 3):
            col_live = [live(right_site, row + SHIFT[s], j) for j in range(3)]
            for i in range(3):
                for j in range(3):
                    r0, c0 = s * D + i * BLOCK, j * BLOCK
                    block = x[slot, r0 : r0 + BLOCK, c0 : c0 + BLOCK].astype(F32)
                    store(s, i * BLOCK, c0, (block * (row_live[i] * col_live[j])).astype(BF16))

    def store_r(s, r0, c0, block):
        right_m[r0 : r0 + BLOCK, s * D + c0 : s * D + c0 + BLOCK] = block

    def store_l(s, r0, c0, block):
        left_m[s * D + r0 : s * D + r0 + BLOCK, c0 : c0 + BLOCK] = block

    mask(1, store_r)
    pl.semaphore_wait(barrier, 5)

    even_r = [
        copy(0, right_m.at[:, cols(1, 2)], halo_low.at[:, cols(0, 2)], (seg, up)),
        copy(1, right_m.at[:, cols(1, 2)], halo_high.at[:, cols(1, 2)], (seg, down)),
        copy(2, right_m.at[:, cols(3)], halo_low.at[:, cols(2)], (seg, up)),
        copy(3, right_m.at[:, cols(0)], halo_high.at[:, cols(0)], (seg, down)),
    ]
    for c in even_r:
        c.start()
    mask(0, store_l)

    def edge_copies(base, left, low, high):
        return [
            copy(base, left.at[3 * D : 4 * D, :], low, (seg, up)),
            copy(base + 1, left.at[0:D, :], high, (seg, down)),
        ]

    def mixed_copies(base, s0, s3, x_ref):
        return [
            copy(base, s0.at[:, cols(0, 2)], x_ref.at[0:D, cols(1, 2)], (seg, down)),
            copy(base + 1, s3.at[:, cols(1, 2)], x_ref.at[3 * D : 4 * D, cols(1, 2)], (seg, up)),
            copy(base + 2, s0.at[:, cols(2)], x_ref.at[0:D, cols(3)], (seg, down)),
            copy(base + 3, s3.at[:, cols(0)], x_ref.at[3 * D : 4 * D, cols(0)], (seg, up)),
        ]

    def zero(ref, where):
        @pl.when(where)
        def _():
            ref[...] = jnp.zeros(ref.shape, ref.dtype)

    def mix(gate, pairs, s0, s3, x_ref):
        def source(s1, s2, r):
            if s1 == 0:
                return theta_0[pl.ds(r, ROWS), cols(s2 - 1)]
            if s1 == 3:
                return theta_3[pl.ds(r, ROWS), cols(s2)]
            return theta_12[pl.ds(r + (s1 - 1) * D, ROWS), cols(s2)]

        def step(i, carry):
            r = pl.multiple_of(i * ROWS, ROWS)
            parts = [source(s1, s2, r) for s1, s2 in pairs]
            for t1, t2 in pairs:
                total = None
                for (s1, s2), part in zip(pairs, parts):
                    term = gate[4 * t1 + t2, 4 * s1 + s2] * part
                    total = term if total is None else total + term
                total = total.astype(BF16)
                if t1 == 0:
                    s0[pl.ds(r, ROWS), cols(t2 - 1)] = total
                elif t1 == 3:
                    s3[pl.ds(r, ROWS), cols(t2)] = total
                else:
                    x_ref[pl.ds(r + t1 * D, ROWS), cols(t2)] = total
            return carry

        lax.fori_loop(0, D // ROWS, step, 0)

    def project(right, x_ref, t, count):
        value = dot_nt(right[...], x_ref[t * D : (t + count) * D, :])
        high, low = split(value)
        proj_r[0:D, cols(t, count)] = high
        proj_r[D : 2 * D, cols(t, count)] = high
        proj_r[2 * D : 3 * D, cols(t, count)] = low

    def inverse_root(mid_site):
        both = dot_nt(proj_r[0:D, :], proj_r[D : 3 * D, :])
        cross = both[:, D : 2 * D]
        gram = both[:, 0:D] + cross + cross.T
        i0 = lax.broadcasted_iota(jnp.int32, (D, D), 0)
        i1 = lax.broadcasted_iota(jnp.int32, (D, D), 1)
        identity = jnp.where(i0 == i1, 1.0, 0.0).astype(F32)
        live_rows = counts[mid_site, row] * BLOCK
        gram = gram + jnp.where((i0 == i1) & (i0 >= live_rows), 1.0, 0.0)
        widest = jnp.max(jnp.sum(jnp.abs(gram), axis=0, keepdims=True), axis=1, keepdims=True)
        ns_s[...] = gram / widest
        for pair in range(3):
            s = ns_s[...]
            store_left(ns_l, s)
            store_right(ns_r, s, 0)
            square = dot(ns_l[...], ns_r[:, 0:D])
            store_right(ns_q, (square - 9.0 * s + 27.0 * identity) * 0.0625, 0)
            store_left(ns_l, square)
            growth = dot(ns_l[...], ns_q[...]) + (36.0 * identity - 39.0 * s) * 0.0625
            store_left(ns_g, growth)
            if pair == 0:
                factor = growth
                moved = dot(ns_g[...], ns_r[:, 0:D])
            elif pair == 1:
                product = dot(ns_g[...], ns_r[...])
                moved, factor = product[:, 0:D], product[:, D : 2 * D]
            else:
                factor = dot(ns_g[...], ns_r[:, D : 2 * D])
            if pair < 2:
                store_right(ns_r, factor, D)
                store_right(ns_q, moved, 0)
                ns_s[...] = dot(ns_g[...], ns_q[...])
        store_left(ns_l, factor / jnp.sqrt(widest))
        new_t[...] = dot(ns_l[...], proj_r[...]).astype(BF16)

    def new_left(dst):
        i0 = lax.broadcasted_iota(jnp.int32, (D, D), 0)
        i1 = lax.broadcasted_iota(jnp.int32, (D, D), 1)
        identity = jnp.where(i0 == i1, 1.0, 0.0).astype(BF16)
        for t in (0, 3, 1, 2):
            dst[t * D : (t + 1) * D, :] = dot_nt(identity, new_t[:, cols(t)]).astype(BF16)

    def new_right(x_ref, store):
        for half in range(2):
            value = dot(new_t[...], x_ref[:, cols(2 * half, 2)]).astype(BF16)
            store(2 * half, value[:, 0:D])
            store(2 * half + 1, value[:, D : 2 * D])

    def bond(gate, mid_site, left, right, low, high, arrivals, edges, sends, e_low, e_high,
             s0, s3, x_ref):
        theta_12[...] = dot(left[D : 3 * D, :], right[...])
        arrivals[0]()
        theta_0[:, cols(0, 2)] = dot(left[0:D, :], low[:, cols(0, 2)])
        arrivals[1]()
        theta_3[:, cols(1, 2)] = dot(left[3 * D : 4 * D, :], high[:, cols(1, 2)])
        mix(gate, MINUS, s0, s3, x_ref)
        sends[0].start()
        mix(gate, PLUS, s0, s3, x_ref)
        sends[1].start()
        arrivals[2]()
        theta_0[:, cols(2)] = dot(left[0:D, :], low[:, cols(2)])
        arrivals[3]()
        theta_3[:, cols(0)] = dot(left[3 * D : 4 * D, :], high[:, cols(0)])
        mix(gate, ZERO, s0, s3, x_ref)
        sends[2].start()
        sends[3].start()
        project(right, x_ref, 1, 2)
        for c in edges:
            c.wait_recv()
        x_ref[0:D, cols(0)] = (gate[0, 0] * dot(e_high[...], right[:, cols(0)])).astype(BF16)
        x_ref[3 * D : 4 * D, cols(3)] = (gate[15, 15] * dot(e_low[...], right[:, cols(3)])).astype(BF16)
        for c in sends:
            c.wait_recv()
        zero(x_ref.at[0:D, :], last)
        zero(x_ref.at[3 * D : 4 * D, :], first)
        project(right, x_ref, 0, 1)
        project(right, x_ref, 3, 1)
        inverse_root(mid_site)

    edges = edge_copies(4, left_m, edge_low, edge_high)
    for c in edges:
        c.start()
    sends = mixed_copies(6, send_0, send_3, mixed)

    def arrive(k, ref, where):
        def wait():
            even_r[k].wait_recv()
            zero(ref, where)
        return wait

    bond(gate_even, 2 * seg + 1, left_m, right_m, halo_low, halo_high,
         [arrive(0, halo_low.at[:, cols(0, 2)], first), arrive(1, halo_high.at[:, cols(1, 2)], last),
          arrive(2, halo_low.at[:, cols(2)], first), arrive(3, halo_high.at[:, cols(0)], last)],
         edges, sends, edge_low, edge_high, send_0, send_3, mixed)

    new_left(new_l)
    back = [
        copy(10, new_l.at[0:D, :], returned.at[0:D, :], (0, up)),
        copy(11, new_l.at[3 * D : 4 * D, :], returned.at[D : 2 * D, :], (0, down)),
    ]
    move = [
        copy(12, new_l.at[D : 2 * D, :], halo_low_o.at[:, cols(0)], (0, up)),
        copy(13, new_l.at[D : 2 * D, :], halo_high_o.at[:, cols(1)], (0, down)),
        copy(14, new_l.at[2 * D : 3 * D, :], halo_low_o.at[:, cols(1)], (0, up)),
        copy(15, new_l.at[2 * D : 3 * D, :], halo_high_o.at[:, cols(2)], (0, down)),
        copy(16, new_l.at[0:D, :], right_o.at[:, cols(0)], (0, up)),
        copy(17, new_l.at[3 * D : 4 * D, :], right_o.at[:, cols(3)], (0, down)),
        copy(18, new_l.at[D : 2 * D, :], right_o.at[:, cols(1)], (0, row)),
        copy(19, new_l.at[2 * D : 3 * D, :], right_o.at[:, cols(2)], (0, row)),
        copy(20, new_l.at[3 * D : 4 * D, :], halo_low_o.at[:, cols(2)], (0, row)),
        copy(21, new_l.at[0:D, :], halo_high_o.at[:, cols(0)], (0, row)),
    ]
    odd_edges = edge_copies(22, left_o, edge_low_o, edge_high_o)
    odd_sends = mixed_copies(24, send_0o, send_3o, mixed_o)
    odd_back = [
        copy(28, new_lo.at[0:D, :], returned_o.at[0:D, :], (0, up)),
        copy(29, new_lo.at[3 * D : 4 * D, :], returned_o.at[D : 2 * D, :], (0, down)),
    ]
    hand_over = copy(30, left_m, right_new, (1, row))

    @pl.when(seg == 1)
    def _():
        for c in move:
            c.start()

        def store(s, value):
            out[1, s * D : (s + 1) * D, :] = value

        new_right(mixed, store)
        for c in move:
            c.wait_send()
        hand_over.wait_recv()
        out[0, :, :] = right_new[...]

    @pl.when(seg == 0)
    def _():
        for c in back:
            c.start()

        def store(s, value):
            left_o[s * D : (s + 1) * D, :] = value

        new_right(mixed, store)
        for c in odd_edges:
            c.start()
        out[0, D : 3 * D, :] = new_l[D : 3 * D, :]

        def arrive_own():
            for k in (4, 5, 6, 7):
                move[k].wait_recv()
            zero(right_o.at[:, cols(0)], first)
            zero(right_o.at[:, cols(3)], last)

        def arrive_low():
            move[0].wait_recv()
            move[2].wait_recv()
            zero(halo_low_o.at[:, cols(0, 2)], first)

        def arrive_high():
            move[1].wait_recv()
            move[3].wait_recv()
            zero(halo_high_o.at[:, cols(1, 2)], last)

        def arrive_low_3():
            move[8].wait_recv()
            zero(halo_low_o.at[:, cols(2)], first)

        def arrive_high_0():
            move[9].wait_recv()
            zero(halo_high_o.at[:, cols(0)], last)

        arrive_own()
        bond(gate_odd, 2, left_o, right_o, halo_low_o, halo_high_o,
             [arrive_low, arrive_high, arrive_low_3, arrive_high_0],
             odd_edges, odd_sends, edge_low_o, edge_high_o, send_0o, send_3o, mixed_o)
        new_left(new_lo)
        for c in odd_back:
            c.start()
        for c in edges:
            c.wait_send()

        def store_new(s, value):
            left_m[s * D : (s + 1) * D, :] = value

        new_right(mixed_o, store_new)
        hand_over.start()
        out[1, D : 3 * D, :] = new_lo[D : 3 * D, :]
        for source, slot, copies in ((returned, 0, back), (returned_o, 1, odd_back)):
            for c in copies:
                c.wait_recv()
            zero(source.at[0:D, :], first)
            zero(source.at[D : 2 * D, :], last)
            out[slot, 0:D, :] = source[0:D, :]
            out[slot, 3 * D : 4 * D, :] = source[D : 2 * D, :]
        for c in back + odd_edges + odd_sends + odd_back + [hand_over]:
            c.wait_send()

    @pl.when(seg == 1)
    def _():
        for c in edges:
            c.wait_send()

    for c in even_r + sends:
        c.wait_send()


def body(site_tensors, block_counts, gate_even, gate_odd):
    sites = site_tensors.shape[0]
    x = site_tensors.reshape(sites, 4 * D, D)
    vmem = pl.BlockSpec(memory_space=pltpu.VMEM)
    smem = pl.BlockSpec(memory_space=pltpu.SMEM)
    unit = lambda r, c, dtype=BF16: pltpu.VMEM((r * D, c * D), dtype)
    phase = [unit(4, 1), unit(1, 4), unit(1, 3), unit(1, 3), unit(1, 1), unit(1, 1),
             unit(1, 3), unit(1, 3), unit(4, 4), unit(2, 1)]
    evolved = pl.pallas_call(
        kernel,
        out_shape=jax.ShapeDtypeStruct(x.shape, x.dtype),
        in_specs=[vmem, smem, smem, smem],
        out_specs=vmem,
        scratch_shapes=phase + phase + [
            unit(4, 1),
            unit(1, 3, F32), unit(2, 4, F32), unit(1, 3, F32),
            unit(3, 4), unit(1, 4), unit(4, 1), unit(4, 1),
            unit(1, 1, F32), unit(1, 3), unit(1, 3), unit(3, 2), unit(3, 1),
            pltpu.SemaphoreType.DMA((31,)), pltpu.SemaphoreType.DMA((31,)),
        ],
        compiler_params=pltpu.CompilerParams(
            collective_id=0, has_side_effects=True, vmem_limit_bytes=60 * 2**20
        ),
    )(x, block_counts, gate_even, gate_odd)
    return evolved.reshape(site_tensors.shape)


def solution(mesh):
    in_specs = (P("seg", "row", None, None, None), P(), P(), P())
    out_specs = P("seg", "row", None, None, None)
    return jax.shard_map(body, mesh=mesh, in_specs=in_specs, out_specs=out_specs, check_vma=False)
```

time: 414 us -> 137 us (0.33)
  the two profiles are of different devices: /device:TPU:127 before, /device:TPU:0 now
where the time goes in v1:
time: 137 us
  Pallas kernels  134 us (98%)
  local copies, waits for them, and re-layouts  3.31 us (2%)
    pallas_call x1, Pallas kernels, body(): pl.pallas_call(kernel, out_shape=jax.ShapeDtypeStruct(x.shape, x.dtype),...  134 us
    unnamed x1, local copies, waits for them, and re-layouts  3.31 us

profile of v1, /device:TPU:0, one launch (start us, length us, event | category | flops | bytes accessed | tf_op | source)
XLA Modules:
  0.0 137.3 jit_solution(8906582732503696737)
XLA Ops:
  0.0 134.0 %shard_map.46 = bf16[2,1536,384]{2,1,0:T(8,128)(2,1)} custom-call(bf16[2,1536,384]{2,1,0:T(8,128)(2,1)} %bitcast.5, s32[4,128]{1,0:T(4,128)} %counts.1, f32[16,16]{1,0:T(8,128)} %gate_even.1, f32[16,16]{1,0:T(8,128)} %gate_odd.1), custom_call_target="tpu_custom_call" | custom-call | tf_op jit(solution)/shard_map/pallas_call | solution.py:377
  134.0 3.3 %copy.7 = bf16[2,1,4,384,384]{4,3,2,1,0:T(8,128)(2,1)} copy(bf16[2,1,4,384,384]{4,3,2,1,0:T(8,128)(2,1)} %bitcast.4) | data formatting | bytes 4718592

commit v2 on v1

v2 whole, which is shorter than its diff:
```python
import functools

import jax
import jax.numpy as jnp
from jax import lax
from jax.experimental import pallas as pl
from jax.experimental.pallas import tpu as pltpu
from jax.sharding import PartitionSpec as P

MESH = pl.DeviceIdType.MESH
BF16, F32 = jnp.bfloat16, jnp.float32
BLOCK = 128
D = 384
SHIFT = (-1, 0, 0, 1)
ROWS = 16

MINUS = ((0, 1), (0, 2), (1, 0), (2, 0))
ZERO = ((0, 3), (1, 1), (1, 2), (2, 1), (2, 2), (3, 0))
PLUS = ((1, 3), (2, 3), (3, 1), (3, 2))


def dot(a, b):
    return jnp.dot(a, b, preferred_element_type=F32)


def dot_nt(a, b):
    return lax.dot_general(a, b, (((1,), (1,)), ((), ())), preferred_element_type=F32)


def split(x):
    high = x.astype(BF16)
    return high, (x - high.astype(F32)).astype(BF16)


def put(ref, x, at=0):
    high, low = split(x)
    ref[0, :, at : at + D] = high
    ref[1, :, at : at + D] = low


def dot3(a, b, start=0, stop=D):
    first, second = a[0, :, 0:D], a[1, :, 0:D]
    left = jnp.concatenate([first, first, second], axis=1)
    high, low = b[0, :, start:stop], b[1, :, start:stop]
    return dot(left, jnp.concatenate([high, low, high], axis=0))


def cols(s, count=1):
    return slice(s * D, (s + count) * D)


PLACE = (2, 0, 1, 3)


def at(t):
    return cols(PLACE[t])


def eye(dtype=F32):
    i0 = lax.broadcasted_iota(jnp.int32, (D, D), 0)
    i1 = lax.broadcasted_iota(jnp.int32, (D, D), 1)
    return jnp.where(i0 == i1, 1.0, 0.0).astype(dtype)


def kernel(x, counts, gate_even, gate_odd, out,
           right_m, halo_low, halo_high, edge_low, edge_high, send_0, send_3, mixed,
           right_o, halo_low_o, halo_high_o, edge_low_o, edge_high_o, send_0o, send_3o, mixed_o,
           x_v, left_m, left_o, new_r, theta_0, theta_12, theta_3, proj_r, new_t, new_l, new_lo,
           ns_rz, ns_q, ns_p, ns_g, send_sem, recv_sem, local_sem, go_sem):
    seg, row = lax.axis_index("seg"), lax.axis_index("row")
    rows = lax.axis_size("row")
    up, down = lax.rem(row + 1, rows), lax.rem(row + rows - 1, rows)

    loads = [pltpu.make_async_copy(x.at[k], x_v.at[k], local_sem.at[k]) for k in (0, 1)]
    loads[1].start()
    loads[0].start()
    barrier = pltpu.get_barrier_semaphore()
    for target in ((seg, up), (seg, down), (1 - seg, row), (1 - seg, up), (1 - seg, down)):
        pl.semaphore_signal(barrier, inc=1, device_id=target, device_id_type=MESH)

    def copy(k, src, dst, target):
        return pltpu.make_async_remote_copy(
            src_ref=src, dst_ref=dst, send_sem=send_sem.at[k], recv_sem=recv_sem.at[k],
            device_id=target, device_id_type=MESH,
        )

    def live(site, sector, block):
        inside = (sector >= 0) & (sector < rows)
        count = counts[site, jnp.clip(sector, 0, rows - 1)]
        return jnp.where(inside & (block < count), 1.0, 0.0).astype(F32)

    def mask(slot, store):
        site = 2 * seg + slot
        right_site = lax.rem(site + 1, 4)
        row_live = [live(site, row, i) for i in range(3)]
        for s in range(4):
            col_live = [live(right_site, row + SHIFT[s], j) for j in range(3)]
            for i in range(3):
                for j in range(3):
                    r0, c0 = s * D + i * BLOCK, j * BLOCK
                    block = x_v[slot, r0 : r0 + BLOCK, c0 : c0 + BLOCK].astype(F32)
                    store(s, i * BLOCK, c0, (block * (row_live[i] * col_live[j])).astype(BF16))

    def store_r(s, r0, c0, block):
        right_m[r0 : r0 + BLOCK, s * D + c0 : s * D + c0 + BLOCK] = block

    def store_l(s, r0, c0, block):
        left_m[s * D + r0 : s * D + r0 + BLOCK, c0 : c0 + BLOCK] = block

    def edge_copies(base, left, low, high):
        return [
            copy(base, left.at[3 * D : 4 * D, :], low, (seg, up)),
            copy(base + 1, left.at[0:D, :], high, (seg, down)),
        ]

    def mixed_copies(base, s0, s3, x_ref):
        return [
            copy(base, s0.at[:, cols(0, 2)], x_ref.at[at(0), cols(1, 2)], (seg, down)),
            copy(base + 1, s3.at[:, cols(1, 2)], x_ref.at[at(3), cols(1, 2)], (seg, up)),
            copy(base + 2, s0.at[:, cols(2)], x_ref.at[at(0), cols(3)], (seg, down)),
            copy(base + 3, s3.at[:, cols(0)], x_ref.at[at(3), cols(0)], (seg, up)),
        ]

    def mix(gate, pairs, right_site, s0, s3, x_ref):
        charge = SHIFT[pairs[0][0]] + SHIFT[pairs[0][1]]
        lane = lax.broadcasted_iota(jnp.int32, (ROWS, D), 1)
        count = counts[right_site, jnp.clip(row + charge, 0, rows - 1)]
        inside = (row + charge >= 0) & (row + charge < rows)
        keep = jnp.where(lane < jnp.where(inside, count, 0) * BLOCK, 1.0, 0.0).astype(F32)
        keep_0 = keep * jnp.where(row > 0, 1.0, 0.0).astype(F32)
        keep_3 = keep * jnp.where(row < rows - 1, 1.0, 0.0).astype(F32)

        def source(s1, s2, r):
            if s1 == 0:
                return theta_0[pl.ds(r, ROWS), cols(s2 - 1)]
            if s1 == 3:
                return theta_3[pl.ds(r, ROWS), cols(s2)]
            return theta_12[pl.ds(r + (s1 - 1) * D, ROWS), cols(s2)]

        def step(i, carry):
            r = pl.multiple_of(i * ROWS, ROWS)
            parts = [source(s1, s2, r) for s1, s2 in pairs]
            for t1, t2 in pairs:
                total = None
                for (s1, s2), part in zip(pairs, parts):
                    term = gate[4 * t1 + t2, 4 * s1 + s2] * part
                    total = term if total is None else total + term
                if t1 == 0:
                    s0[pl.ds(r, ROWS), cols(t2 - 1)] = (total * keep_0).astype(BF16)
                elif t1 == 3:
                    s3[pl.ds(r, ROWS), cols(t2)] = (total * keep_3).astype(BF16)
                else:
                    x_ref[pl.ds(r + PLACE[t1] * D, ROWS), cols(t2)] = (total * keep).astype(BF16)
            return carry

        lax.fori_loop(0, D // ROWS, step, 0)

    def store_projected(value, where):
        high, low = split(value)
        proj_r[0:D, where] = high
        proj_r[D : 2 * D, where] = high
        proj_r[2 * D : 3 * D, where] = low

    def gram_part(where):
        return dot_nt(proj_r[0:D, where], proj_r[D : 3 * D, where])

    def inverse_root(both, mid_site):
        identity = eye()
        cross = both[:, D : 2 * D]
        gram = both[:, 0:D] + cross + cross.T
        i0 = lax.broadcasted_iota(jnp.int32, (D, D), 0)
        gram = gram + jnp.where(i0 >= counts[mid_site, row] * BLOCK, identity, 0.0)
        widest = jnp.max(jnp.sum(jnp.abs(gram), axis=0, keepdims=True), axis=1, keepdims=True)
        s = gram / widest
        for pair in range(3):
            put(ns_rz, s)
            square = dot3(ns_rz, ns_rz)
            put(ns_q, (square - 9.0 * s + 27.0 * identity) * 0.0625)
            put(ns_p, square)
            growth = dot3(ns_p, ns_q) + (36.0 * identity - 39.0 * s) * 0.0625
            put(ns_g, growth)
            if pair == 0:
                factor, moved = growth, dot3(ns_g, ns_rz)
            elif pair == 1:
                product = dot3(ns_g, ns_rz, 0, 2 * D)
                moved, factor = product[:, 0:D], product[:, D : 2 * D]
            else:
                factor = dot3(ns_g, ns_rz, D, 2 * D)
            if pair < 2:
                put(ns_rz, factor, D)
                put(ns_q, moved)
                s = dot3(ns_g, ns_q)
        high, low = split(factor / jnp.sqrt(widest))
        left = jnp.concatenate([high, low, high], axis=1)
        new_t[...] = dot(left, proj_r[...]).astype(BF16)

    def new_left(dst, order):
        identity = eye(BF16)
        for t in order:
            dst[cols(t), :] = dot_nt(identity, new_t[:, at(t)]).astype(BF16)

    def new_right(x_ref, dst):
        for half in range(2):
            value = dot(new_t[...], x_ref[:, cols(2 * half, 2)]).astype(BF16)
            dst[cols(2 * half), :] = value[:, 0:D]
            dst[cols(2 * half + 1), :] = value[:, D : 2 * D]

    def bond(gate, mid_site, right_site, left, right, low, high, arrivals, edges, sends,
             e_low, e_high, s0, s3, x_ref, before_root):
        theta_12[:, cols(0)] = dot(left[cols(1, 2), :], right[:, cols(0)])
        arrivals[0]()
        theta_0[:, cols(0, 2)] = dot(left[cols(0), :], low[:, cols(0, 2)])
        mix(gate, MINUS, right_site, s0, s3, x_ref)
        sends[0].start()
        theta_12[:, cols(3)] = dot(left[cols(1, 2), :], right[:, cols(3)])
        arrivals[1]()
        theta_3[:, cols(1, 2)] = dot(left[cols(3), :], high[:, cols(1, 2)])
        mix(gate, PLUS, right_site, s0, s3, x_ref)
        sends[1].start()
        theta_12[:, cols(1, 2)] = dot(left[cols(1, 2), :], right[:, cols(1, 2)])
        arrivals[2]()
        theta_0[:, cols(2)] = dot(left[cols(0), :], low[:, cols(2)])
        arrivals[3]()
        theta_3[:, cols(0)] = dot(left[cols(3), :], high[:, cols(0)])
        mix(gate, ZERO, right_site, s0, s3, x_ref)
        sends[2].start()
        sends[3].start()
        inner, outer = cols(0, 2), cols(2, 2)
        store_projected(dot_nt(right[...], x_ref[inner, :]), inner)
        theta_12[0:D, cols(0, 2)] = gram_part(inner)
        for c in edges:
            c.wait_recv()
        x_ref[at(0), cols(0)] = (gate[0, 0] * dot(e_high[...], right[:, cols(0)])).astype(BF16)
        x_ref[at(3), cols(3)] = (gate[15, 15] * dot(e_low[...], right[:, cols(3)])).astype(BF16)
        for c in sends[:2]:
            c.wait_recv()
        theta_0[:, cols(0)] = dot_nt(right[:, cols(0, 3)], x_ref[at(0), cols(0, 3)])
        theta_3[:, cols(0)] = dot_nt(right[:, cols(1, 3)], x_ref[at(3), cols(1, 3)])
        sends[2].wait_recv()
        last_0 = dot_nt(right[:, cols(3)], x_ref[at(0), cols(3)])
        store_projected(theta_0[:, cols(0)] + last_0, at(0))
        sends[3].wait_recv()
        last_3 = dot_nt(right[:, cols(0)], x_ref[at(3), cols(0)])
        store_projected(theta_3[:, cols(0)] + last_3, at(3))
        before_root()
        inverse_root(theta_12[0:D, cols(0, 2)] + gram_part(outer), mid_site)

    xs = [x.at[1, cols(s), :] for s in range(4)]
    even_r = [
        copy(0, xs[1], halo_low.at[:, cols(0)], (seg, up)),
        copy(1, xs[2], halo_low.at[:, cols(1)], (seg, up)),
        copy(2, xs[1], halo_high.at[:, cols(1)], (seg, down)),
        copy(3, xs[2], halo_high.at[:, cols(2)], (seg, down)),
        copy(4, xs[3], halo_low.at[:, cols(2)], (seg, up)),
        copy(5, xs[0], halo_high.at[:, cols(0)], (seg, down)),
    ]
    edges = edge_copies(6, left_m, edge_low, edge_high)
    sends = mixed_copies(8, send_0, send_3, mixed)

    def start_even():
        for k in (0, 2, 1, 3, 4, 5):
            even_r[k].start()

    def arrive(*which):
        def wait():
            for k in which:
                even_r[k].wait_recv()
        return wait

    def wait_both(k):
        def wait():
            even_r[k].wait_recv()
            @pl.when(seg == 1)
            def _():
                pl.semaphore_signal(go_sem, inc=1, device_id=(0, row), device_id_type=MESH)
        return wait

    pl.semaphore_wait(barrier, 5)

    @pl.when(seg == 1)
    def _():
        start_even()

    loads[1].wait()
    mask(1, store_r)
    loads[0].wait()
    mask(0, store_l)

    @pl.when(seg == 0)
    def _():
        pl.semaphore_wait(go_sem, 1)
        start_even()

    for c in edges:
        c.start()
    bond(gate_even, 2 * seg + 1, lax.rem(2 * seg + 2, 4), left_m, right_m, halo_low, halo_high,
         [arrive(0, 1), arrive(2, 3), arrive(4), wait_both(5)], edges, sends,
         edge_low, edge_high, send_0, send_3, mixed, lambda: None)

    back = [
        copy(12, new_l.at[cols(0), :], out.at[0, cols(0), :], (0, up)),
        copy(13, new_l.at[cols(3), :], out.at[0, cols(3), :], (0, down)),
    ]
    move = [
        copy(14, new_l.at[cols(1), :], halo_low_o.at[:, cols(0)], (0, up)),
        copy(15, new_l.at[cols(2), :], halo_low_o.at[:, cols(1)], (0, up)),
        copy(16, new_l.at[cols(1), :], halo_high_o.at[:, cols(1)], (0, down)),
        copy(17, new_l.at[cols(2), :], halo_high_o.at[:, cols(2)], (0, down)),
        copy(18, new_l.at[cols(0), :], right_o.at[:, cols(0)], (0, up)),
        copy(19, new_l.at[cols(3), :], right_o.at[:, cols(3)], (0, down)),
        copy(20, new_l.at[cols(1), :], right_o.at[:, cols(1)], (0, row)),
        copy(21, new_l.at[cols(2), :], right_o.at[:, cols(2)], (0, row)),
        copy(22, new_l.at[cols(3), :], halo_low_o.at[:, cols(2)], (0, row)),
        copy(23, new_l.at[cols(0), :], halo_high_o.at[:, cols(0)], (0, row)),
    ]
    odd_edges = edge_copies(24, left_o, edge_low_o, edge_high_o)
    odd_sends = mixed_copies(26, send_0o, send_3o, mixed_o)
    odd_back = [
        copy(30, new_lo.at[cols(0), :], out.at[1, cols(0), :], (0, up)),
        copy(31, new_lo.at[cols(3), :], out.at[1, cols(3), :], (0, down)),
    ]
    hand_over = [
        copy(32 + h, new_r.at[cols(2 * h, 2), :], out.at[0, cols(2 * h, 2), :], (1, row))
        for h in range(2)
    ]

    @pl.when(seg == 1)
    def _():
        new_left(new_l, (0, 3, 1, 2))
        for k in (4, 5, 0, 2, 1, 3, 6, 7, 8, 9):
            move[k].start()
        new_right(mixed, new_r)
        keep = pltpu.make_async_copy(new_r, out.at[1], local_sem.at[2])
        keep.start()
        for c in hand_over:
            c.wait_recv()
        for c in move:
            c.wait_send()
        keep.wait()

    @pl.when(seg == 0)
    def _():
        new_right(mixed, left_o)
        for c in odd_edges:
            c.start()
        new_left(new_l, (0, 3, 1, 2))
        keep = pltpu.make_async_copy(new_l.at[cols(1, 2), :], out.at[0, cols(1, 2), :], local_sem.at[2])
        keep.start()

        def arrive_odd(*which):
            def wait():
                for k in which:
                    move[k].wait_recv()
            return wait

        def start_back():
            for c in back:
                c.start()

        arrive_odd(4, 5, 6, 7)()
        bond(gate_odd, 2, 3, left_o, right_o, halo_low_o, halo_high_o,
             [arrive_odd(0, 1), arrive_odd(2, 3), arrive_odd(8), arrive_odd(9)],
             odd_edges, odd_sends, edge_low_o, edge_high_o, send_0o, send_3o, mixed_o, start_back)
        new_left(new_lo, (0, 3))
        for c in odd_back:
            c.start()
        for half in range(2):
            value = dot(new_t[...], mixed_o[:, cols(2 * half, 2)]).astype(BF16)
            new_r[cols(2 * half), :] = value[:, 0:D]
            new_r[cols(2 * half + 1), :] = value[:, D : 2 * D]
            hand_over[half].start()
        new_left(new_lo, (1, 2))
        keep_o = pltpu.make_async_copy(new_lo.at[cols(1, 2), :], out.at[1, cols(1, 2), :], local_sem.at[3])
        keep_o.start()
        for c in back + odd_back:
            c.wait_recv()
        for c in back + odd_edges + odd_sends + odd_back + hand_over:
            c.wait_send()
        keep.wait()
        keep_o.wait()

    for c in even_r + edges + sends:
        c.wait_send()


def body(site_tensors, block_counts, gate_even, gate_odd):
    sites = site_tensors.shape[0]
    x = site_tensors.reshape(sites, 4 * D, D)
    hbm = pl.BlockSpec(memory_space=pl.ANY)
    smem = pl.BlockSpec(memory_space=pltpu.SMEM)
    unit = lambda r, c, dtype=BF16: pltpu.VMEM((r * D, c * D), dtype)
    pair = lambda c: pltpu.VMEM((2, D, c * D), BF16)
    phase = [unit(1, 4), unit(1, 3), unit(1, 3), unit(1, 1), unit(1, 1),
             unit(1, 3), unit(1, 3), unit(4, 4)]
    evolved = pl.pallas_call(
        kernel,
        out_shape=jax.ShapeDtypeStruct(x.shape, x.dtype),
        in_specs=[hbm, smem, smem, smem],
        out_specs=hbm,
        scratch_shapes=phase + phase + [
            pltpu.VMEM((2, 4 * D, D), BF16), unit(4, 1), unit(4, 1), unit(4, 1),
            unit(1, 3, F32), unit(2, 4, F32), unit(1, 3, F32),
            unit(3, 4), unit(1, 4), unit(4, 1), unit(4, 1),
            pair(2), pair(1), pair(1), pair(1),
            pltpu.SemaphoreType.DMA((34,)), pltpu.SemaphoreType.DMA((34,)),
            pltpu.SemaphoreType.DMA((4,)), pltpu.SemaphoreType.REGULAR,
        ],
        compiler_params=pltpu.CompilerParams(
            collective_id=0, has_side_effects=True, vmem_limit_bytes=60 * 2**20
        ),
    )(x, block_counts, gate_even, gate_odd)
    return evolved.reshape(site_tensors.shape)


def solution(mesh):
    in_specs = (P("seg", "row", None, None, None), P(), P(), P())
    out_specs = P("seg", "row", None, None, None)
    return jax.shard_map(body, mesh=mesh, in_specs=in_specs, out_specs=out_specs, check_vma=False)
```

time: 137 us -> 114 us (0.83); the launches traced: 137 us -> 112 us
  Pallas kernels: 134 us -> 109 us
    pallas_call x1, Pallas kernels: 134 us -> 109 us  [body(): pl.pallas_call(kernel, out_shape=jax.ShapeDtypeStruct(x.shape, x.dtype),...]
where the time goes in v2:
time: 114 us; the launch traced here: 112 us
  Pallas kernels  109 us (96%)
  local copies, waits for them, and re-layouts  3.31 us (3%)
    pallas_call x1, Pallas kernels, body(): pl.pallas_call(kernel, out_shape=jax.ShapeDtypeStruct(x.shape, x.dtype),...  109 us
    unnamed x1, local copies, waits for them, and re-layouts  3.31 us

profile of v2, /device:TPU:0, one launch (start us, length us, event | category | flops | bytes accessed | tf_op | source)
XLA Modules:
  0.0 112.2 jit_solution(15773393197396294935)
XLA Ops:
  0.0 108.9 %shard_map.46 = bf16[2,1536,384]{2,1,0:T(8,128)(2,1)} custom-call(bf16[2,1536,384]{2,1,0:T(8,128)(2,1)} %bitcast.5, s32[4,128]{1,0:T(4,128)} %counts.1, f32[16,16]{1,0:T(8,128)} %gate_even.1, f32[16,16]{1,0:T(8,128)} %gate_odd.1), custom_call_target="tpu_custom_call" | custom-call | tf_op jit(solution)/shard_map/pallas_call | solution.py:395
  108.9 3.3 %copy.7 = bf16[2,1,4,384,384]{4,3,2,1,0:T(8,128)(2,1)} copy(bf16[2,1,4,384,384]{4,3,2,1,0:T(8,128)(2,1)} %bitcast.4) | data formatting | bytes 4718592
